TPU v7x, 128 devices: a whole 4x4x4 slice. The times are simulated.
128 devices in a mesh: section: 8 (over z_lo, x), uly: 4 (over y), blk: 4 (over z_hi, core).
Axes of the slice: x: 4, y: 4, z: 4 (z_hi: 2, z_lo: 2; z = z_hi * 2 + z_lo), core: 2. Of those that a mesh axis runs over, the one named last changes fastest.
Arguments:
- in_flight: bfloat16 [8, 1024, 3072], P('section', ('uly', 'blk')), may hold values from -6 to 6
- entering: bfloat16 [1, 1024, 3072], P(None, ('uly', 'blk')), may hold values from -6 to 6
- patch_ids: int32 [9], replicated, may hold values from 0 to 3
- timestep: int32 [1], replicated, may hold values from 0 to 49
- time_table: float32 [50, 3072], replicated, may hold values from -6 to 6
- mod_weight: bfloat16 [8, 3072, 3, 3072], P('section', None, None, ('uly', 'blk')), may hold values from -0.109375 to 0.109375
- qkv_weight: bfloat16 [8, 3072, 3, 1536], P('section', None, None, 'uly'), may hold values from -0.109375 to 0.109375
- out_weight: bfloat16 [8, 1536, 3072], P('section', ('uly', 'blk')), may hold values from -0.15625 to 0.15625
- stale_cache: bfloat16 [8, 4096, 2, 1536], P('section', 'blk', None, 'uly'), may hold values from -300 to 300
Outputs:
- outputs: bfloat16 [8, 2, 1024, 3072], P('section', None, ('uly', 'blk'))
All inputs are finite; a program needn't handle non-finite values.
Results may differ from a plain program's by a relative error of at most 0.015.
Values may be sent and summed in bfloat16 or wider, within the bound.
No kernel may reach another device: no remote copies, remote signals or barrier semaphores. Data moves between devices by JAX's collectives and lax.ppermute only.
A program may use at most 128 MiB of HBM per device.

v0:
```python
import jax
import jax.numpy as jnp
from jax import lax
from jax.sharding import PartitionSpec as P

HD = 128


def from_behind(x, axis, by):
    size = lax.axis_size(axis)
    pairs = [(i, i + by) for i in range(size) if 0 <= i + by < size]
    return lax.ppermute(x, axis, pairs)


def normalize_heads(values):
    return values * lax.rsqrt(jnp.mean(values * values, axis=-1, keepdims=True) + 1e-06)


def per_device(
    in_flight,
    entering,
    patch_ids,
    timestep,
    time_table,
    mod_weight,
    qkv_weight,
    out_weight,
    stale_cache,
):
    section_index = lax.axis_index("section")
    section_count = lax.axis_size("section")
    model_width = in_flight.shape[2]
    head_cols = qkv_weight.shape[3]
    local_heads = head_cols // HD
    scale_factor = HD ** (-0.5)
    steps_range = lax.iota(jnp.int32, time_table.shape[0])
    time_vector = jnp.sum(jnp.where((steps_range == timestep[0])[:, None], time_table, 0.0), axis=0)
    activated = jax.nn.silu(time_vector).astype(jnp.bfloat16)
    mod_cols = mod_weight.shape[3]
    mod_part = jnp.dot(
        activated,
        mod_weight[0].reshape(model_width, 3 * mod_cols),
        preferred_element_type=jnp.float32,
    ).reshape(3, mod_cols)
    modulation = lax.all_gather(mod_part, ("uly", "blk"), axis=1, tiled=True)
    weight_flat = qkv_weight[0].reshape(model_width, 3 * head_cols)
    out_rows = lax.all_gather(out_weight[0], ("uly", "blk"), axis=0, tiled=True)
    stale_rows = lax.all_gather(stale_cache[0], "blk", axis=0, tiled=True)
    stale_count = stale_rows.shape[0]
    stale_keys = stale_rows[:, 0].reshape(stale_count, local_heads, HD)
    stale_values = stale_rows[:, 1].reshape(stale_count, local_heads, HD)
    micro_count = entering.shape[0] + 1
    current = in_flight[0]
    results = []
    for tick_index in range(micro_count):
        patch_index = lax.dynamic_index_in_dim(
            patch_ids, tick_index + section_count - 1 - section_index, 0, keepdims=False
        )
        inputs_f = current.astype(jnp.float32)
        center = inputs_f - jnp.mean(inputs_f, axis=-1, keepdims=True)
        normed = center * lax.rsqrt(jnp.mean(center * center, axis=-1, keepdims=True) + 1e-06)
        modulated = (normed * (1.0 + modulation[1]) + modulation[0]).astype(jnp.bfloat16)
        projected = jnp.dot(
            lax.all_gather(modulated, "uly", axis=0, tiled=True),
            weight_flat,
            preferred_element_type=jnp.float32,
        )
        group_rows = projected.shape[0]
        projected = projected.reshape(group_rows, 3, local_heads, HD)
        queries = normalize_heads(projected[:, 0]).astype(jnp.bfloat16)
        keys_new = normalize_heads(projected[:, 1]).astype(jnp.bfloat16)
        values_new = projected[:, 2].astype(jnp.bfloat16)
        fresh = jnp.stack([keys_new, values_new], axis=1).reshape(group_rows, 2, head_cols)
        fresh_all = lax.all_gather(fresh, "blk", axis=0, tiled=True)
        patch_rows = fresh_all.shape[0]
        fresh_keys = fresh_all[:, 0].reshape(patch_rows, local_heads, HD)
        fresh_values = fresh_all[:, 1].reshape(patch_rows, local_heads, HD)
        fresh_scores = (
            jnp.einsum("qhd,khd->hqk", queries, fresh_keys, preferred_element_type=jnp.float32)
            * scale_factor
        )
        allowed = lax.iota(jnp.int32, stale_count) // patch_rows != patch_index
        stale_scores = (
            jnp.einsum("qhd,khd->hqk", queries, stale_keys, preferred_element_type=jnp.float32)
            * scale_factor
        )
        stale_scores = jnp.where(allowed[None, None, :], stale_scores, -1e30)
        peak = jnp.maximum(jnp.max(fresh_scores, axis=-1), jnp.max(stale_scores, axis=-1))
        fresh_weights = jnp.exp(fresh_scores - peak[:, :, None])
        stale_weights = jnp.exp(stale_scores - peak[:, :, None])
        total = jnp.sum(fresh_weights, axis=-1) + jnp.sum(stale_weights, axis=-1)
        numer = jnp.einsum(
            "hqk,khd->qhd",
            fresh_weights.astype(jnp.bfloat16),
            fresh_values,
            preferred_element_type=jnp.float32,
        )
        numer = numer + jnp.einsum(
            "hqk,khd->qhd",
            stale_weights.astype(jnp.bfloat16),
            stale_values,
            preferred_element_type=jnp.float32,
        )
        mixed = numer / jnp.transpose(total)[:, :, None]
        attended = mixed.astype(jnp.bfloat16).reshape(group_rows, head_cols)
        token_heads = lax.all_to_all(attended, "uly", split_axis=0, concat_axis=1, tiled=True)
        branch_out = jnp.dot(token_heads, out_rows, preferred_element_type=jnp.float32)
        block_out = (inputs_f + modulation[2] * branch_out).astype(jnp.bfloat16)
        results.append(block_out)
        if tick_index + 1 < micro_count:
            passed = from_behind(block_out, "section", 1)
            current = jnp.where(section_index == 0, entering[tick_index], passed)
    return jnp.stack(results)[None]


def solution(mesh):
    return jax.shard_map(
        per_device,
        mesh=mesh,
        in_specs=(
            P("section", ("uly", "blk"), None),
            P(None, ("uly", "blk"), None),
            P(),
            P(),
            P(),
            P("section", None, None, ("uly", "blk")),
            P("section", None, None, "uly"),
            P("section", ("uly", "blk"), None),
            P("section", "blk", None, "uly"),
        ),
        out_specs=P("section", None, ("uly", "blk"), None),
        check_vma=False,
    )
```

profile of v0, /device:TPU:0, one launch (start us, length us, event | category | flops | bytes accessed | tf_op | source)
XLA Modules:
  0.0 346.5 jit_solution(15309427404763604460)
XLA Ops:
  9.8 25.5 %all-gather.2 = f32[16,192,3]{1,2,0:T(4,128)S(1)} all-gather(f32[1,192,3]{1,2,0:T(4,128)S(1)} %bitcast.188), channel_id=1, replica_groups=mesh['section'=8,'uly'=4,'blk'=4] {'uly','blk'}, dimensions={0}, use_global_device_ids=true | all-gather | bytes 39168 | tf_op jit(solution)/shard_map/all_gather | solution.py:45
  40.0 10.3 %copy.35 = bf16[1,3072,3,384]{1,3,2,0:T(8,128)(2,1)} copy(bf16[1,3072,3,384]{3,1,2,0:T(8,128)(2,1)} %param.15) | data formatting | bytes 14155776 | tf_op args[6]
  50.3 13.1 %all-gather.10.cloned.1.call-done = bf16[256,3072]{1,0:T(8,128)(2,1)} async-done(((bf16[64,3072]{1,0:T(8,128)(2,1)}), bf16[256,3072]{1,0:T(8,128)(2,1)}) %all-gather.10.cloned.1.call-update) | async-done | bytes 1572880 | tf_op jit(solution)/shard_map/all_gather | solution.py:64
  63.4 5.5 %fusion.49 = f32[256,3,3,128]{0,3,2,1:T(8,128)S(1)} fusion(bf16[3,3,128,3072]{3,2,1,0:T(8,128)(2,1)} %bitcast.164, bf16[256,3072]{1,0:T(8,128)(2,1)} %all-gather.10.cloned.1.call-done), kind=kOutput, calls=%fused_computation.39 | convolution fusion | flops 1811939328 | bytes 9830400 | tf_op jit(solution)/shard_map/dot_general | solution.py:63
  70.9 3.6 %copy.38 = bf16[1,1024,2,384]{1,3,2,0:T(8,128)(2,1)} copy(bf16[1,1024,2,384]{3,2,1,0:T(2,128)(2,1)S(1)} %copy-done.10) | data formatting | bytes 3145728 | tf_op args[8]
  76.8 17.3 %all-gather.12.cloned.1.call-done = bf16[1024,2,384]{0,2,1:T(8,128)(2,1)} async-done(((bf16[256,2,384]{0,2,1:T(8,128)(2,1)}), bf16[1024,2,384]{0,2,1:T(8,128)(2,1)}) %all-gather.12.cloned.1.call-update) | async-done | bytes 1572880 | tf_op jit(solution)/shard_map/all_gather | solution.py:74
  98.8 46.9 %all-gather.18.cloned.1.call-done = bf16[1,4096,2,384]{1,3,2,0:T(8,128)(2,1)} async-done(((bf16[1,1024,2,384]{1,3,2,0:T(8,128)(2,1)}), bf16[1,4096,2,384]{1,3,2,0:T(8,128)(2,1)}) %all-gather.18.cloned.1.call-update) | async-done | bytes 6291472 | tf_op jit(solution)/shard_map/all_gather | solution.py:48
  145.6 3.6 %fusion.113 = (bf16[4096,1,384]{0,2,1:T(8,128)(2,1)S(1)}, bf16[4096,1,384]{0,2,1:T(8,128)(2,1)S(1)}) fusion(bf16[4096,2,384]{0,2,1:T(8,128)(2,1)} %bitcast.166), kind=kLoop, calls=%fused_computation.122 | loop fusion | bytes 12582912 | tf_op jit(solution)/shard_map/slice | solution.py:50
  149.3 3.8 %fusion = (f32[3,256]{1,0:T(4,128)S(1)}, f32[3,256,4096]{2,1,0:T(8,128)S(1)}) fusion(pred[4096]{0:T(1024)(128)(4,1)S(1)} %fusion.105, bf16[4096,3,128]{0,2,1:T(8,128)(2,1)S(1)} %bitcast.162, f32[256,3,3,128]{0,3,2,1:T(8,128)} %copy-done.6, f32[256,3]{0,1:T(4,128)S(1)} %add_rsqrt_fusion.2), kind=kOutput, calls=%fused_computation.4 | convolution fusion | flops 814939392 | bytes 16132096 | tf_op jit(solution)/shard_map/qhd,khd->hqk/dot_general | solution.py:84
  153.8 3.0 fusion.2
  157.6 6.7 %fusion.73 = f32[256,3,128]{0,2,1:T(8,128)S(1)} fusion(bf16[4096,3,128]{0,2,1:T(8,128)(2,1)S(1)} %bitcast.167, f32[3,256,4096]{2,1,0:T(8,128)} %copy-done.2, f32[3,256]{1,0:T(4,128)S(1)} %max.14, pred[4096]{0:T(1024)(128)(4,1)S(1)} %fusion.105), kind=kOutput, calls=%fused_computation.51 | convolution fusion | flops 817889280 | bytes 16129024 | tf_op jit(solution)/shard_map/hqk,khd->qhd/dot_general | solution.py:98
  169.5 10.7 %all_to_all.38 = bf16[4,64,384]{2,1,0:T(8,128)(2,1)S(1)} all-to-all(bf16[4,64,384]{2,1,0:T(8,128)(2,1)} %all_to_all.28), channel_id=1, replica_groups=mesh['section'=8,'uly'=4,'blk'=4] {'uly'}, dimensions={0} | all-to-all | bytes 393216 | tf_op jit(solution)/shard_map/all_to_all | solution.py:106
  180.8 43.5 %all-gather.20.cloned.1.call-done = bf16[1,1536,3072]{2,1,0:T(8,128)(2,1)} async-done(((bf16[1,96,3072]{2,1,0:T(8,128)(2,1)}), bf16[1,1536,3072]{2,1,0:T(8,128)(2,1)}) %all-gather.20.cloned.1.call-update) | async-done | bytes 9437200 | tf_op jit(solution)/shard_map/all_gather | solution.py:47
  224.3 6.3 %fusion.30 = bf16[64,3072]{1,0:T(8,128)(2,1)} fusion(bf16[64,1536]{1,0:T(8,128)(2,1)} %bitcast.171, bf16[1,1536,3072]{2,1,0:T(8,128)(2,1)} %all-gather.20.cloned.1.call-done, bf16[1,64,3072]{2,1,0:T(8,128)(2,1)S(1)} %copy-done.4, f32[3072]{0:T(1024)S(1)} %bitcast.182), kind=kOutput, calls=%fused_computation.24 | convolution fusion | flops 604766208 | bytes 10432512 | tf_op jit(solution)/shard_map/dot_general | solution.py:107
  230.6 4.1 %collective-permute-start = (bf16[64,3072]{1,0:T(8,128)(2,1)}, bf16[64,3072]{1,0:T(8,128)(2,1)}, u32[]{:S(2)}, u32[]{:S(2)}) collective-permute-start(bf16[64,3072]{1,0:T(8,128)(2,1)} %fusion.30), channel_id=1, source_target_pairs={{0,16},{16,32},{32,48},{48,64},{64,80},{80,96},{96,112},{1,17},{17... | collective-permute-start | bytes 1179656 | tf_op jit(solution)/shard_map/ppermute | solution.py:12
  234.7 8.4 %collective-permute-done = bf16[64,3072]{1,0:T(8,128)(2,1)} collective-permute-done((bf16[64,3072]{1,0:T(8,128)(2,1)}, bf16[64,3072]{1,0:T(8,128)(2,1)}, u32[]{:S(2)}, u32[]{:S(2)}) %collective-permute-start) | collective-permute-done | bytes 393248 | tf_op jit(solution)/shard_map/ppermute | solution.py:12
  246.6 25.2 %all-gather.14.cloned.1.call-done = bf16[256,3072]{1,0:T(8,128)(2,1)} async-done(((bf16[64,3072]{1,0:T(8,128)(2,1)}), bf16[256,3072]{1,0:T(8,128)(2,1)}) %all-gather.14.cloned.1.call-update) | async-done | bytes 1572880 | tf_op jit(solution)/shard_map/all_gather | solution.py:64
  271.7 5.6 %fusion.47 = f32[256,3,3,128]{0,3,2,1:T(8,128)S(1)} fusion(bf16[3,3,128,3072]{3,2,1,0:T(8,128)(2,1)} %bitcast.165, bf16[256,3072]{1,0:T(8,128)(2,1)} %all-gather.14.cloned.1.call-done), kind=kOutput, calls=%fused_computation.37 | convolution fusion | flops 1811939328 | bytes 9830400 | tf_op jit(solution)/shard_map/dot_general | solution.py:63
  280.8 7.8 %fusion.1 = (f32[3,256]{1,0:T(4,128)S(1)}, f32[3,256,4096]{2,1,0:T(8,128)}) fusion(pred[4096]{0:T(1024)(128)(4,1)S(1)} %fusion.104, bf16[4096,3,128]{0,2,1:T(8,128)(2,1)S(1)} %bitcast.163, f32[256,3,3,128]{0,3,2,1:T(8,128)} %copy-done.7, f32[256,3]{0,1:T(4,128)S(1)} %add_rsqrt_fusion), kind=kOutput, calls=%fused_computation.5 | convolution fusion | flops 814939392 | bytes 16132096 | tf_op jit(solution)/shard_map/qhd,khd->hqk/dot_general | solution.py:84
  288.6 14.7 %all-gather.16.cloned.1.call-done = bf16[1024,2,384]{0,2,1:T(8,128)(2,1)} async-done(((bf16[256,2,384]{0,2,1:T(8,128)(2,1)}), bf16[1024,2,384]{0,2,1:T(8,128)(2,1)}) %all-gather.16.cloned.1.call-update) | async-done | bytes 1572880 | tf_op jit(solution)/shard_map/all_gather | solution.py:74
  306.7 6.5 %fusion.76 = f32[256,3,128]{0,2,1:T(8,128)S(1)} fusion(bf16[4096,3,128]{0,2,1:T(8,128)(2,1)S(1)} %bitcast.168, f32[3,256,4096]{2,1,0:T(8,128)} %get-tuple-element.25, f32[3,256]{1,0:T(4,128)S(1)} %max.15, pred[4096]{0:T(1024)(128)(4,1)S(1)} %fusion.104), kind=kOutput, calls=%fused_computation.52 | convolution fusion | flops 817889280 | bytes 16129024 | tf_op jit(solution)/shard_map/hqk,khd->qhd/dot_general | solution.py:98
  313.2 6.5 %fusion.4 = f32[3,256]{1,0:T(4,128)S(1)} fusion(f32[3,256,4096]{2,1,0:T(8,128)} %get-tuple-element.25, f32[3,256]{1,0:T(4,128)S(1)} %max.15, pred[4096]{0:T(1024)(128)(4,1)S(1)} %fusion.104), kind=kLoop, calls=%fused_computation.8 | loop fusion | flops 12582144 | bytes 12593152 | tf_op jit(solution)/shard_map/reduce_sum | solution.py:91
  321.6 10.5 %all_to_all.39 = bf16[4,64,384]{2,1,0:T(8,128)(2,1)S(1)} all-to-all(bf16[4,64,384]{2,1,0:T(8,128)(2,1)S(1)} %all_to_all.32), channel_id=1, replica_groups=mesh['section'=8,'uly'=4,'blk'=4] {'uly'}, dimensions={0} | all-to-all | bytes 393216 | tf_op jit(solution)/shard_map/all_to_all | solution.py:106
  332.1 5.7 %fusion.36 = bf16[1,64,3072]{2,1,0:T(8,128)(2,1)S(1)} fusion(bf16[64,1536]{1,0:T(8,128)(2,1)S(1)} %bitcast.172, bf16[1,1536,3072]{2,1,0:T(8,128)(2,1)} %all-gather.20.cloned.1.call-done, bf16[64,3072]{1,0:T(8,128)(2,1)} %copy-done.5, f32[3072]{0:T(1024)S(1)} %bitcast.183), kind=kOutput, calls=%fused_computation.26 | convolution fusion | flops 604766208 | bytes 10432512 | tf_op jit(solution)/shard_map/dot_general | solution.py:107
  (97 shorter events, 37.3 us)
Async XLA Ops:
  6.5 2.3 copy-start
  6.5 56.8 %all-gather.10.cloned.1.call-start = ((), (), s32[]{:S(2)}) async-start(), calls=%async_computation.2 | async-start | bytes 1966080 | tf_op jit(solution)/shard_map/all_gather | solution.py:64
  35.5 14.8 %copy-start.12 = (f32[1,3072]{1,0:T(1,128)}, f32[1,3072]{1,0:T(1,128)S(1)}, u32[]{:S(2)}) copy-start(f32[1,3072]{1,0:T(1,128)S(1)} %get-tuple-element.14) | copy-start | bytes 36868
  35.5 14.8 %copy-start.13 = (f32[1,3072]{1,0:T(1,128)}, f32[1,3072]{1,0:T(1,128)S(1)}, u32[]{:S(2)}) copy-start(f32[1,3072]{1,0:T(1,128)S(1)} %get-tuple-element.15) | copy-start | bytes 36868
  39.9 54.2 %all-gather.12.cloned.1.call-start = ((), (), s32[]{:S(2)}) async-start(), calls=%async_computation.3 | async-start | bytes 1966080 | tf_op jit(solution)/shard_map/all_gather | solution.py:74
  68.9 27.6 %copy-start.6 = (f32[256,3,3,128]{0,3,2,1:T(8,128)}, f32[256,3,3,128]{0,3,2,1:T(8,128)S(1)}, u32[]{:S(2)}) copy-start(f32[256,3,3,128]{0,3,2,1:T(8,128)S(1)} %fusion.49) | copy-start | bytes 3538948
  68.9 2.0 copy-start.10
  69.1 6.3 %copy-start.14 = (s32[9]{0:T(128)S(1)}, s32[9]{0:T(128)}, u32[]{:S(2)}) copy-start(s32[9]{0:T(128)} %param.11) | copy-start | bytes 112
  69.9 75.7 %all-gather.18.cloned.1.call-start = ((), (), s32[]{:S(2)}) async-start(), calls=%async_computation.6 | async-start | bytes 7864320 | tf_op jit(solution)/shard_map/all_gather | solution.py:48
  74.6 149.7 %all-gather.20.cloned.1.call-start = ((), (), s32[]{:S(2)}) async-start(), calls=%async_computation.7 | async-start | bytes 10027008 | tf_op jit(solution)/shard_map/all_gather | solution.py:47
  75.1 196.6 %all-gather.14.cloned.1.call-start = ((), (), s32[]{:S(2)}) async-start(), calls=%async_computation.4 | async-start | bytes 1966080 | tf_op jit(solution)/shard_map/all_gather | solution.py:64
  149.2 8.4 %copy-start.8 = (bf16[4096,1,384]{0,2,1:T(8,128)(2,1)}, bf16[4096,1,384]{0,2,1:T(8,128)(2,1)S(1)}, u32[]{:S(2)}) copy-start(bf16[4096,1,384]{0,2,1:T(8,128)(2,1)S(1)} %get-tuple-element.8) | copy-start | bytes 9437188
  149.3 3.8 %copy-start.3 = (f32[3,256,1024]{2,1,0:T(8,128)S(1)}, f32[3,256,1024]{2,1,0:T(8,128)}, u32[]{:S(2)}) copy-start(f32[3,256,1024]{2,1,0:T(8,128)} %get-tuple-element.19) | copy-start | bytes 9437188
  153.0 4.6 %copy-start.2 = (f32[3,256,4096]{2,1,0:T(8,128)}, f32[3,256,4096]{2,1,0:T(8,128)S(1)}, u32[]{:S(2)}) copy-start(f32[3,256,4096]{2,1,0:T(8,128)S(1)} %get-tuple-element.21) | copy-start | bytes 37748740
  157.6 6.7 %copy-start.11 = (bf16[1024,1,384]{0,2,1:T(8,128)(2,1)S(1)}, bf16[1024,1,384]{0,2,1:T(8,128)(2,1)}, u32[]{:S(2)}) copy-start(bf16[1024,1,384]{0,2,1:T(8,128)(2,1)} %get-tuple-element.11) | copy-start | bytes 2359300
  164.4 59.9 %copy-start.4 = (bf16[1,64,3072]{2,1,0:T(8,128)(2,1)S(1)}, bf16[1,64,3072]{2,1,0:T(8,128)(2,1)}, u32[]{:S(2)}) copy-start(bf16[1,64,3072]{2,1,0:T(8,128)(2,1)} %param.9) | copy-start | bytes 1179652
  230.6 12.5 %collective-permute-start = (bf16[64,3072]{1,0:T(8,128)(2,1)}, bf16[64,3072]{1,0:T(8,128)(2,1)}, u32[]{:S(2)}, u32[]{:S(2)}) collective-permute-start(bf16[64,3072]{1,0:T(8,128)(2,1)} %fusion.30), channel_id=1, source_target_pairs={{0,16},{16,32},{32,48},{48,64},{64,80},{80,96},{96,112},{1,17},{17... | collective-permute-start | bytes 1179656 | tf_op jit(solution)/shard_map/ppermute | solution.py:12
  244.3 33.0 %copy-start.5 = (bf16[64,3072]{1,0:T(8,128)(2,1)}, bf16[64,3072]{1,0:T(8,128)(2,1)S(1)}, u32[]{:S(2)}) copy-start(bf16[64,3072]{1,0:T(8,128)(2,1)S(1)} %get-tuple-element.6) | copy-start | bytes 1179652
  246.3 57.1 %all-gather.16.cloned.1.call-start = ((), (), s32[]{:S(2)}) async-start(), calls=%async_computation.5 | async-start | bytes 1966080 | tf_op jit(solution)/shard_map/all_gather | solution.py:74
  277.3 1.0 copy-start.7
  303.4 3.4 copy-start.9
  332.1 7.6 %copy-start.1 = (bf16[1,3072,3,192]{1,3,2,0:T(8,128)(2,1)S(1)}, bf16[1,3072,3,192]{1,3,2,0:T(8,128)(2,1)}, u32[]{:S(2)}) copy-start(bf16[1,3072,3,192]{1,3,2,0:T(8,128)(2,1)} %param.14) | copy-start | bytes 10616836
Sparse Core Ops, SparseCore 0:
  40.1 23.2 all-gather.9
  70.0 24.0 all-gather.11
  95.8 49.7 all-gather.17
  147.9 76.3 all-gather.19
  246.4 25.2 all-gather.13
  279.3 24.0 all-gather.15
where the time goes:
time: 348 us; the launch traced here: 347 us
  waiting for transfers between devices  170 us (49%)
  matrix products  55.1 us (16%)
  blocking collectives  46.6 us (13%)
  local copies, waits for them, and re-layouts  29.9 us (9%)
  other arithmetic  26.1 us (8%)
  between operations  14.6 us (4%)
  starting transfers between devices  4.71 us (1%)
    all_gather x1, waiting for transfers between devices, per_device(): stale_rows = lax.all_gather(stale_cache[0], 'blk', axis=0, tiled=True)  46.9 us
    all_gather x1, waiting for transfers between devices, per_device(): out_rows = lax.all_gather(out_weight[0], ('uly', 'blk'), axis=0, tiled=True)  43.5 us
    all_gather x2, waiting for transfers between devices, per_device(): lax.all_gather(modulated, 'uly', axis=0, tiled=True)  38.2 us
    all_gather x2, waiting for transfers between devices, per_device(): fresh_all = lax.all_gather(fresh, 'blk', axis=0, tiled=True)  32.1 us
    all_gather x1, blocking collectives, per_device(): modulation = lax.all_gather(mod_part, ('uly', 'blk'), axis=1, tiled=True)  25.5 us
    all_to_all x2, blocking collectives, per_device(): lax.all_to_all(attended, 'uly', split_axis=0, concat_axis=1, tiled=True)  21.1 us
    unnamed x33, local copies, waits for them, and re-layouts  16.8 us
    dot_general x2, matrix products, per_device(): jnp.einsum('hqk,khd->qhd', stale_weights.astype(jnp.bfloat16), stale_valu...  13.2 us
  transfers between devices with their start and end apart: 7, of which 7 were waited for; matrix products, arithmetic and copies ran while one was open for 15% of the time, Pallas kernels for 0%

commit v1 on v0

v1 whole, which is shorter than its diff:
```python
import functools

import jax
import jax.numpy as jnp
from jax import lax
from jax.experimental import pallas as pl
from jax.experimental.pallas import tpu as pltpu
from jax.sharding import PartitionSpec as P

HD = 128
F32 = jnp.float32
BF16 = jnp.bfloat16
LOG2E = 1.4426950408889634
VMEM_BYTES = 48 * 1024 * 1024
SMEM_SPEC = pl.BlockSpec(memory_space=pltpu.SMEM)
VMEM_SPEC = pl.BlockSpec(memory_space=pltpu.VMEM)


def shift(x, section=0, uly=0, blk=0):
    names = ("section", "uly", "blk")
    moves = (section, uly, blk)
    used = tuple(n for n, m in zip(names, moves) if m)
    sizes = [lax.axis_size(n) for n in used]
    total = 1
    for size in sizes:
        total *= size
    pairs = []
    for source in range(total):
        rest, place = source, []
        for size in reversed(sizes):
            place.insert(0, rest % size)
            rest //= size
        target = 0
        for name, size, at in zip(used, sizes, place):
            move = moves[names.index(name)]
            target = target * size + ((at ^ move) if name == "blk" else (at + move) % size)
        pairs.append((source, target))
    return lax.ppermute(x, used if len(used) > 1 else used[0], pairs)


def params():
    return pltpu.CompilerParams(vmem_limit_bytes=VMEM_BYTES)


def norm_rows(x, mod_ref):
    center = x - jnp.mean(x, axis=-1, keepdims=True)
    normed = center * lax.rsqrt(jnp.mean(center * center, axis=-1, keepdims=True) + 1e-06)
    return (normed * (1.0 + mod_ref[1:2, :]) + mod_ref[0:1, :]).astype(BF16)


def norm_heads(part, heads):
    out = []
    for h in range(heads):
        v = part[:, h * HD : (h + 1) * HD]
        out.append(v * lax.rsqrt(jnp.mean(v * v, axis=-1, keepdims=True) + 1e-06))
    return jnp.concatenate(out, axis=1).astype(BF16)


def project_step(mod_s, w_ref, q_ref, k_ref, v_ref):
    g = pl.program_id(0)
    part = jnp.dot(mod_s[...], w_ref[0], preferred_element_type=F32)
    heads = part.shape[1] // HD

    @pl.when(g == 0)
    def _():
        q_ref[...] = norm_heads(part, heads)

    @pl.when(g == 1)
    def _():
        k_ref[...] = norm_heads(part, heads)

    @pl.when(g == 2)
    def _():
        v_ref[...] = part.astype(BF16)


def qkv_first_kernel(n, sc, x0, x1, x2, x3, mod_ref, w_ref, q_ref, k_ref, v_ref, cols_ref, mod_s):
    u = sc[1]
    rows = x0.shape[0]
    width = cols_ref.shape[1]

    @pl.when(pl.program_id(0) == 0)
    def _():
        for k, ref in enumerate((x0, x1, x2, x3)):
            at = pl.multiple_of(lax.rem(u - k + n, n) * rows, rows)
            mod_s[pl.ds(at, rows), :] = norm_rows(ref[...].astype(F32), mod_ref)
            cols_ref[pl.ds(at, rows), :] = ref[:, pl.ds(pl.multiple_of(u * width, 128), width)]

    project_step(mod_s, w_ref, q_ref, k_ref, v_ref)


def qkv_next_kernel(
    n, sc, y0, y1, y2, y3, enter, mod_ref, w_ref, q_ref, k_ref, v_ref, ret_ref, own_ref, mod_s, x_s
):
    u = sc[1]
    first = sc[0] == 0
    width = y0.shape[1]
    rows = own_ref.shape[0]

    @pl.when(pl.program_id(0) == 0)
    def _():
        for k, ref in enumerate((y0, y1, y2, y3)):
            at = pl.multiple_of(lax.rem(u - k + n, n) * width, 128)
            x_s[:, pl.ds(at, width)] = ref[...]
        mine = pl.ds(pl.multiple_of(u * rows, rows), rows)
        ret_ref[...] = x_s[mine, :]

        @pl.when(first)
        def _():
            x_s[...] = enter[...]

        own_ref[...] = x_s[mine, :]
        for r in range(n):
            mod_s[r * rows : (r + 1) * rows, :] = norm_rows(
                x_s[r * rows : (r + 1) * rows, :].astype(F32), mod_ref
            )

    project_step(mod_s, w_ref, q_ref, k_ref, v_ref)


def fixed(shape):
    return pl.BlockSpec(shape, lambda *g: (0,) * len(shape))


def qkv_first(n, scalars, pieces, modulation, weight):
    rows, width = pieces[0].shape
    cols = weight.shape[2]
    tokens = n * rows
    out = jax.ShapeDtypeStruct((tokens, cols), BF16)
    return pl.pallas_call(
        functools.partial(qkv_first_kernel, n),
        grid=(3,),
        in_specs=[SMEM_SPEC]
        + [fixed((rows, width))] * 4
        + [fixed(modulation.shape), pl.BlockSpec((1, width, cols), lambda g: (g, 0, 0))],
        out_specs=[fixed((tokens, cols))] * 3 + [fixed((tokens, width // n))],
        out_shape=[out] * 3 + [jax.ShapeDtypeStruct((tokens, width // n), BF16)],
        scratch_shapes=[pltpu.VMEM((tokens, width), BF16)],
        compiler_params=params(),
        name="qkv_first",
    )(scalars, *pieces, modulation, weight)


def qkv_next(n, scalars, pieces, enter, modulation, weight):
    tokens, part = pieces[0].shape
    width = part * n
    cols = weight.shape[2]
    rows = tokens // n
    out = jax.ShapeDtypeStruct((tokens, cols), BF16)
    return pl.pallas_call(
        functools.partial(qkv_next_kernel, n),
        grid=(3,),
        in_specs=[SMEM_SPEC]
        + [fixed((tokens, part))] * 4
        + [fixed(enter.shape), fixed(modulation.shape)]
        + [pl.BlockSpec((1, width, cols), lambda g: (g, 0, 0))],
        out_specs=[fixed((tokens, cols))] * 3 + [fixed((rows, width))] * 2,
        out_shape=[out] * 3 + [jax.ShapeDtypeStruct((rows, width), BF16)] * 2,
        scratch_shapes=[pltpu.VMEM((tokens, width), BF16)] * 2,
        compiler_params=params(),
        name="qkv_next",
    )(scalars, *pieces, enter, modulation, weight)


def attend_kernel(packed, sc, patch, q_ref, ko, vo, km, vm, so, sm, *outs):
    b = sc[2]
    p = patch[0]
    heads = q_ref.shape[1] // HD
    rows = q_ref.shape[0]
    rate = HD ** (-0.5) * LOG2E
    lane = lax.broadcasted_iota(jnp.int32, (rows, HD), 1)
    stats = jnp.zeros((rows, HD), F32)
    nt = (((1,), (1,)), ((), ()))
    for h in range(heads):
        at = slice(h * HD, (h + 1) * HD)
        q = q_ref[:, at]
        scores = []
        for keys in (ko[:, at], km[:, at], so[0, :, at], sm[0, :, at]):
            scores.append(lax.dot_general(q, keys, nt, preferred_element_type=F32))
        scores[2] = jnp.where(p == b, -1e30, scores[2])
        scores[3] = jnp.where(p == jnp.bitwise_xor(b, 1), -1e30, scores[3])
        peak = functools.reduce(
            jnp.maximum, [jnp.max(s, axis=-1, keepdims=True) for s in scores]
        )
        total = jnp.zeros((rows, 1), F32)
        numer = jnp.zeros((rows, HD), F32)
        for s, values in zip(scores, (vo[:, at], vm[:, at], so[1, :, at], sm[1, :, at])):
            weights = jnp.exp2((s - peak) * rate)
            total = total + jnp.sum(weights, axis=-1, keepdims=True)
            numer = numer + jnp.dot(weights.astype(BF16), values, preferred_element_type=F32)
        mixed = numer / total
        level = peak * rate + jnp.log2(total)
        if packed:
            outs[0][:, at] = mixed.astype(BF16)
            high = level.astype(BF16).astype(F32)
            middle = (level - high).astype(BF16).astype(F32)
            low = level - high - middle
            for j, part in enumerate((high, middle, low)):
                stats = jnp.where(lane == 3 * h + j, part, stats)
        else:
            outs[0][:, at] = mixed
            stats = jnp.where(lane == h, level, stats)
    if packed:
        outs[0][:, heads * HD :] = stats.astype(BF16)
    else:
        outs[1][...] = stats


def attend(packed, scalars, patch, q, ko, vo, km, vm, so, sm):
    rows, cols = q.shape
    if packed:
        out_shape = [jax.ShapeDtypeStruct((rows, cols + HD), BF16)]
    else:
        out_shape = [jax.ShapeDtypeStruct((rows, cols), F32), jax.ShapeDtypeStruct((rows, HD), F32)]
    return pl.pallas_call(
        functools.partial(attend_kernel, packed),
        in_specs=[SMEM_SPEC] * 2 + [VMEM_SPEC] * 7,
        out_specs=[VMEM_SPEC] * len(out_shape),
        out_shape=out_shape,
        compiler_params=params(),
        name="attend_other" if packed else "attend_own",
    )(scalars, patch, q, ko, vo, km, vm, so, sm)


def merge_kernel(o_ref, level_ref, other_ref, out_ref):
    cols = o_ref.shape[1]
    for h in range(cols // HD):
        at = slice(h * HD, (h + 1) * HD)
        mine = level_ref[:, h : h + 1]
        parts = [
            other_ref[:, cols + 3 * h + j : cols + 3 * h + j + 1].astype(F32) for j in range(3)
        ]
        theirs = parts[0] + parts[1] + parts[2]
        peak = jnp.maximum(mine, theirs)
        a, b = jnp.exp2(mine - peak), jnp.exp2(theirs - peak)
        mixed = (a * o_ref[:, at] + b * other_ref[:, at].astype(F32)) / (a + b)
        out_ref[:, at] = mixed.astype(BF16)


def merge(o, level, other):
    return pl.pallas_call(
        merge_kernel,
        in_specs=[VMEM_SPEC] * 3,
        out_specs=VMEM_SPEC,
        out_shape=jax.ShapeDtypeStruct(o.shape, BF16),
        compiler_params=params(),
        name="merge",
    )(o, level, other)


def place_kernel(n, sc, w_ref, out_ref):
    u, b = sc[1], sc[2]
    rows = w_ref.shape[1]
    for j, flip in enumerate((0, 2, 1, 3)):
        for k in range(n):
            at = lax.rem(u - k + n, n) * 4 + jnp.bitwise_xor(b, flip)
            out_ref[pl.ds(pl.multiple_of(at * rows, rows), rows), :] = w_ref[j * n + k]


def place(n, scalars, pieces):
    count, rows, cols = pieces.shape
    return pl.pallas_call(
        functools.partial(place_kernel, n),
        in_specs=[SMEM_SPEC, VMEM_SPEC],
        out_specs=VMEM_SPEC,
        out_shape=jax.ShapeDtypeStruct((count * rows, cols), BF16),
        compiler_params=params(),
        name="place",
    )(scalars, pieces)


def out_cols_kernel(n, sc, a0, a1, a2, a3, w_ref, x_ref, gate_ref, y_ref):
    u = sc[1]
    depth = a0.shape[1]
    total = None
    for k, ref in enumerate((a0, a1, a2, a3)):
        at = pl.multiple_of(lax.rem(u - k + n, n) * depth, 128)
        part = jnp.dot(ref[...], w_ref[pl.ds(at, depth), :], preferred_element_type=F32)
        total = part if total is None else total + part
    y_ref[...] = (x_ref[...].astype(F32) + gate_ref[...] * total).astype(BF16)


def out_cols(n, scalars, pieces, weight, x, gate):
    return pl.pallas_call(
        functools.partial(out_cols_kernel, n),
        in_specs=[SMEM_SPEC] + [VMEM_SPEC] * 7,
        out_specs=VMEM_SPEC,
        out_shape=jax.ShapeDtypeStruct(x.shape, BF16),
        compiler_params=params(),
        name="out_cols",
    )(scalars, *pieces, weight, x, gate)


def out_last_kernel(n, sc, a0, a1, a2, a3, w_ref, x_ref, mod_ref, before_ref, y_ref):
    u = sc[1]
    depth = a0.shape[1]
    total = None
    for k, ref in enumerate((a0, a1, a2, a3)):
        at = pl.multiple_of(lax.rem(u + k, n) * depth, 128)
        part = jnp.dot(ref[...], w_ref[pl.ds(at, depth), :], preferred_element_type=F32)
        total = part if total is None else total + part
    y_ref[0, 0] = before_ref[...]
    y_ref[0, 1] = (x_ref[...].astype(F32) + mod_ref[2:3, :] * total).astype(BF16)


def out_last(n, scalars, pieces, weight, x, modulation, before):
    rows, width = x.shape
    chunk = width // 4
    return pl.pallas_call(
        functools.partial(out_last_kernel, n),
        grid=(width // chunk,),
        in_specs=[SMEM_SPEC]
        + [fixed(pieces[0].shape)] * 4
        + [pl.BlockSpec((weight.shape[0], chunk), lambda g: (0, g))]
        + [pl.BlockSpec((rows, chunk), lambda g: (0, g))]
        + [pl.BlockSpec((3, chunk), lambda g: (0, g))]
        + [pl.BlockSpec((rows, chunk), lambda g: (0, g))],
        out_specs=pl.BlockSpec((1, 2, rows, chunk), lambda g: (0, 0, 0, g)),
        out_shape=jax.ShapeDtypeStruct((1, 2, rows, width), BF16),
        compiler_params=params(),
        name="out_last",
    )(scalars, *pieces, weight, x, modulation, before)


def per_device(
    in_flight,
    entering,
    patch_ids,
    timestep,
    time_table,
    mod_weight,
    qkv_weight,
    out_weight,
    stale_cache,
):
    s = lax.axis_index("section")
    u = lax.axis_index("uly")
    b = lax.axis_index("blk")
    n = lax.axis_size("uly")
    section_count = lax.axis_size("section")
    rows, width = in_flight.shape[1:]
    part = width // n
    scalars = jnp.stack([s, u, b]).astype(jnp.int32)
    patches = [lax.dynamic_slice(patch_ids, (t + section_count - 1 - s,), (1,)) for t in range(2)]

    x_pieces = [in_flight[0]] + [shift(in_flight[0], uly=k) for k in range(1, n)]
    time_vector = lax.dynamic_index_in_dim(time_table, timestep[0], 0, keepdims=False)
    activated = jax.nn.silu(time_vector).astype(BF16)
    mod_cols = mod_weight.shape[3]
    mod_part = jnp.dot(
        activated, mod_weight[0].reshape(width, 3 * mod_cols), preferred_element_type=F32
    ).reshape(3, mod_cols)
    group = n * lax.axis_size("blk")
    spread = lax.all_to_all(
        jnp.broadcast_to(mod_part[None], (group, 3, mod_cols)), ("uly", "blk"), 0, 0
    )
    modulation = jnp.transpose(spread, (1, 0, 2)).reshape(3, width)

    weight = jnp.transpose(qkv_weight[0], (1, 0, 2))
    stale_own = jnp.transpose(stale_cache[0], (1, 0, 2))
    stale_mate = shift(stale_own, blk=1)

    w_cut = [
        lax.dynamic_slice(out_weight[0], (0, lax.rem(u + k, n) * part), (out_weight.shape[1], part))
        for k in range(n)
    ]
    w_pieces = jnp.stack([shift(w_cut[k], section=1, uly=k) for k in range(n)])
    w_two = jnp.concatenate([w_pieces, shift(w_pieces, blk=2)], axis=0)
    w_four = jnp.concatenate([w_two, shift(w_two, blk=1)], axis=0)
    w_before = place(n, scalars, w_four)

    q, k_new, v_new, cols = qkv_first(n, scalars, x_pieces, modulation, weight)
    cols_before = shift(cols, section=1)
    gate_before = shift(modulation[2:3], section=1)
    gate_part = lax.dynamic_slice(gate_before, (0, u * part), (1, part))
    enter_all = lax.all_gather(entering[0], "uly", axis=0, tiled=True)
    out_rows = lax.all_gather(out_weight[0], ("uly", "blk"), axis=0, tiled=True)

    def attention(q, k_new, v_new, patch):
        q_other = shift(q, blk=2)
        k_mate, v_mate = shift(k_new, blk=1), shift(v_new, blk=1)
        rest = (k_new, v_new, k_mate, v_mate, stale_own, stale_mate)
        o, level = attend(False, scalars, patch, q, *rest)
        (for_other,) = attend(True, scalars, patch, q_other, *rest)
        return merge(o, level, shift(for_other, blk=2))

    attended = attention(q, k_new, v_new, patches[0])
    a_pieces = [shift(attended, section=1, uly=k) for k in range(n)]
    y = out_cols(n, scalars, a_pieces, w_before, cols_before, gate_part)
    y_pieces = [y] + [shift(y, uly=k) for k in range(1, n)]
    q, k_new, v_new, back, x_own = qkv_next(n, scalars, y_pieces, enter_all, modulation, weight)
    before = shift(back, section=-1)
    attended = attention(q, k_new, v_new, patches[1])

    def tokens_of(k):
        return lax.dynamic_slice(attended, (lax.rem(u - k + n, n) * rows, 0), (rows, attended.shape[1]))

    last = [tokens_of(0)] + [shift(tokens_of(k), uly=-k) for k in range(1, n)]
    return out_last(n, scalars, last, out_rows, x_own, modulation, before)


def solution(mesh):
    return jax.shard_map(
        per_device,
        mesh=mesh,
        in_specs=(
            P("section", ("uly", "blk"), None),
            P(None, ("uly", "blk"), None),
            P(),
            P(),
            P(),
            P("section", None, None, ("uly", "blk")),
            P("section", None, None, "uly"),
            P("section", ("uly", "blk"), None),
            P("section", "blk", None, "uly"),
        ),
        out_specs=P("section", None, ("uly", "blk"), None),
        check_vma=False,
    )
```

time: 348 us -> 254 us (0.73)
  waiting for transfers between devices: 170 us -> 102 us
  Pallas kernels: 0 us -> 57.5 us
  matrix products: 55.1 us -> 1.91 us
  blocking collectives: 46.6 us -> 0 us
  starting transfers between devices: 4.71 us -> 41.1 us
  other arithmetic: 26.1 us -> 0.15 us
  local copies, waits for them, and re-layouts: 29.9 us -> 34.9 us
    all_gather x5 -> x1, waiting for transfers between devices: 117 us -> 0.01 us  [per_device(): enter_all = lax.all_gather(entering[0], 'uly', axis=0, tiled=True)]
    ppermute x1 -> x31, waiting for transfers between devices: 8.35 us -> 79.3 us  [shift(): return lax.ppermute(x, used if len(used) > 1 else used[0], pairs)]
    pallas_call x0 -> x11, Pallas kernels: none -> 57.5 us  [the longest x4 25.6 us: attend(): pl.pallas_call(functools.partial(attend_kernel, packed), in_specs=[SMEM_S...]
    dot_general x13 -> x1, matrix products: 55.1 us -> 1.91 us  [per_device(): jnp.dot(activated, mod_weight[0].reshape(width, 3 * mod_cols), preferred_...]
    all_gather x1, waiting for transfers between devices: 43.5 us -> 0.01 us  [per_device(): out_rows = lax.all_gather(out_weight[0], ('uly', 'blk'), axis=0, tiled=True)]
    ppermute x1 -> x31, starting transfers between devices: 4.1 us -> 34.9 us  [shift(): return lax.ppermute(x, used if len(used) > 1 else used[0], pairs)]
    all_gather x1 -> x0, blocking collectives: 25.5 us -> none  [per_device(): modulation = lax.all_gather(mod_part, ('uly', 'blk'), axis=1, tiled=True)]
    all_to_all x2 -> x0, blocking collectives: 21.1 us -> none  [per_device(): lax.all_to_all(attended, 'uly', split_axis=0, concat_axis=1, tiled=True)]
  transfers between devices with their start and end apart: 7 -> 34, of which waited for: 7 -> 18; matrix products, arithmetic and copies ran while one was open for 15% -> 8% of each run, Pallas kernels for 0% -> 20%
where the time goes in v1:
time: 254 us; the launch traced here: 252 us
  waiting for transfers between devices  102 us (40%)
  Pallas kernels  57.5 us (23%)
  starting transfers between devices  41.1 us (16%)
  local copies, waits for them, and re-layouts  34.9 us (14%)
  between operations  14.3 us (6%)
    ppermute x31, waiting for transfers between devices, shift(): return lax.ppermute(x, used if len(used) > 1 else used[0], pairs)  79.3 us
    ppermute x31, starting transfers between devices, shift(): return lax.ppermute(x, used if len(used) > 1 else used[0], pairs)  34.9 us
    pallas_call x4, Pallas kernels, attend(): pl.pallas_call(functools.partial(attend_kernel, packed), in_specs=[SMEM_S...  25.6 us
    unnamed x55, local copies, waits for them, and re-layouts  22.4 us
    all_to_all x1, waiting for transfers between devices, per_device(): lax.all_to_all(jnp.broadcast_to(mod_part[None], (group, 3, mod_cols)), ('...  21.1 us
    pallas_call x1, Pallas kernels, qkv_first(): pl.pallas_call(functools.partial(qkv_first_kernel, n), grid=(3,), in_spec...  9.15 us
    pallas_call x1, Pallas kernels, qkv_next(): pl.pallas_call(functools.partial(qkv_next_kernel, n), grid=(3,), in_specs...  8 us
    all_to_all x1, starting transfers between devices, per_device(): lax.all_to_all(jnp.broadcast_to(mod_part[None], (group, 3, mod_cols)), ('...  6.15 us
  transfers between devices with their start and end apart: 34, of which 18 were waited for; matrix products, arithmetic and copies ran while one was open for 8% of the time, Pallas kernels for 20%

profile of v1, /device:TPU:0, one launch (start us, length us, event | category | flops | bytes accessed | tf_op | source)
XLA Modules:
  0.0 251.7 jit_solution(16463312030465428225)
XLA Ops:
  13.4 3.5 %collective-permute-start.14 = (bf16[96,768]{1,0:T(8,128)(2,1)S(1)}, bf16[96,768]{1,0:T(8,128)(2,1)S(1)}, u32[]{:S(2)}, u32[]{:S(2)}) collective-permute-start(bf16[96,768]{1,0:T(8,128)(2,1)S(1)} %get-tuple-element.34), channel_id=1, source_target_pairs={{0,24},{4,28},{8,16},{12,20},{16,40},{20,44},{24,32},{28,36},{32,5... | collective-permute-start | bytes 442376 | tf_op jit(solution)/shard_map/ppermute | solution.py:38
  19.5 2.8 %copy.16 = bf16[1,1024,2,384]{3,1,2,0:T(8,128)(2,1)} copy(bf16[1,1024,2,384]{3,2,1,0:T(2,128)(2,1)} %param.17) | data formatting | bytes 3145728 | tf_op args[8]
  23.8 4.5 %collective-permute-done.14 = bf16[96,768]{1,0:T(8,128)(2,1)S(1)} collective-permute-done((bf16[96,768]{1,0:T(8,128)(2,1)S(1)}, bf16[96,768]{1,0:T(8,128)(2,1)S(1)}, u32[]{:S(2)}, u32[]{:S(2)}) %collective-permute-start.14) | collective-permute-done | bytes 147488 | tf_op jit(solution)/shard_map/ppermute | solution.py:38
  29.5 3.7 %collective-permute-start.16 = (bf16[4,96,768]{2,1,0:T(8,128)(2,1)S(1)}, bf16[4,96,768]{2,1,0:T(8,128)(2,1)S(1)}, u32[]{:S(2)}, u32[]{:S(2)}) collective-permute-start(bf16[4,96,768]{2,1,0:T(8,128)(2,1)S(1)} %pad_maximum_fusion), channel_id=1, source_target_pairs={{0,2},{1,3},{2,0},{3,1},{4,6},{5,7},{6,4},{7,5},{8,10},{9,11},{10,... | collective-permute-start | bytes 1769480 | tf_op jit(solution)/shard_map/ppermute | solution.py:38
  36.1 9.4 %collective-permute-done.16 = bf16[4,96,768]{2,1,0:T(8,128)(2,1)S(1)} collective-permute-done((bf16[4,96,768]{2,1,0:T(8,128)(2,1)S(1)}, bf16[4,96,768]{2,1,0:T(8,128)(2,1)S(1)}, u32[]{:S(2)}, u32[]{:S(2)}) %collective-permute-start.16) | collective-permute-done | bytes 589856 | tf_op jit(solution)/shard_map/ppermute | solution.py:38
  53.9 6.2 %all-to-all-start = ((f32[16,3,192]{2,1,0:T(4,128)}), f32[16,3,192]{2,1,0:T(4,128)}, u32[]{:S(2)}, u32[]{:S(2)}) async-start(f32[16,3,192]{2,1,0:T(4,128)} %broadcast_in_dim.2), calls=%async_computation | async-start | bytes 131072 | tf_op jit(solution)/shard_map/all_to_all | solution.py:354
  60.2 21.1 %all-to-all-done = f32[16,3,192]{2,1,0:T(4,128)} async-done(((f32[16,3,192]{2,1,0:T(4,128)}), f32[16,3,192]{2,1,0:T(4,128)}, u32[]{:S(2)}, u32[]{:S(2)}) %all-to-all-start) | async-done | bytes 36896 | tf_op jit(solution)/shard_map/all_to_all | solution.py:354
  85.1 9.2 %qkv_first.1 = (bf16[256,384]{1,0:T(8,128)(2,1)}, bf16[256,384]{1,0:T(8,128)(2,1)}, bf16[256,384]{1,0:T(8,128)(2,1)}, bf16[256,768]{1,0:T(8,128)(2,1)}) custom-call(s32[3]{0:T(128)S(1)} %pad_add_fusion.sc, bf16[64,3072]{1,0:T(8,128)(2,1)} %bitcast.3.x0, bf16[64,3072]{1,0:T(8,128)(2,1)} %collective-permute-done.x1, ...), custom_call_target="tpu_custom_call" | custom-call | tf_op jit(solution)/shard_map/qkv_first/pallas_call | solution.py:130
  96.3 12.0 %collective-permute-done.6.q_ref = bf16[256,384]{1,0:T(8,128)(2,1)} collective-permute-done((bf16[256,384]{1,0:T(8,128)(2,1)}, bf16[256,384]{1,0:T(8,128)(2,1)}, u32[]{:S(2)}, u32[]{:S(2)}) %collective-permute-start.6) | collective-permute-done | bytes 196640 | tf_op jit(solution)/shard_map/ppermute | solution.py:38
  108.3 7.0 %attend_other.2 = bf16[256,512]{1,0:T(8,128)(2,1)} custom-call(s32[3]{0:T(128)S(1)} %pad_add_fusion.sc, s32[1]{0:T(128)} %get-tuple-element.49.patch, bf16[256,384]{1,0:T(8,128)(2,1)} %collective-permute-done.6.q_ref, bf16[256,384]{1,0:T(8,128)(2,1)} %get-tuple-element.19.ko, bf16[256,384]{1,0:T(8,128)(2,1)} %get-tuple-element.20.vo, ...), custom_call_target="tpu_custom_call" | custom-call | tf_op jit(solution)/shard_map/attend_other/pallas_call | solution.py:215
  117.7 6.2 %attend_own.2 = (f32[256,384]{1,0:T(8,128)S(1)}, f32[256,128]{1,0:T(8,128)S(1)}) custom-call(s32[3]{0:T(128)S(1)} %pad_add_fusion.sc, s32[1]{0:T(128)} %get-tuple-element.49.patch, bf16[256,384]{1,0:T(8,128)(2,1)} %get-tuple-element.18.q_ref, bf16[256,384]{1,0:T(8,128)(2,1)} %get-tuple-element.19.ko, bf16[256,384]{1,0:T(8,128)(2,1)} %get-tuple-element.20.vo, ...), custom_call_target="tpu_custom_call" | custom-call | tf_op jit(solution)/shard_map/attend_own/pallas_call | solution.py:215
  124.0 9.5 %collective-permute-done.7.other_ref = bf16[256,512]{1,0:T(8,128)(2,1)} collective-permute-done((bf16[256,512]{1,0:T(8,128)(2,1)}, bf16[256,512]{1,0:T(8,128)(2,1)}, u32[]{:S(2)}, u32[]{:S(2)}) %collective-permute-start.7) | collective-permute-done | bytes 262176 | tf_op jit(solution)/shard_map/ppermute | solution.py:38
  135.7 7.9 %collective-permute-start.9 = (bf16[256,384]{1,0:T(8,128)(2,1)S(1)}, bf16[256,384]{1,0:T(8,128)(2,1)S(1)}, u32[]{:S(2)}, u32[]{:S(2)}) collective-permute-start(bf16[256,384]{1,0:T(8,128)(2,1)S(1)} %merge.2), channel_id=1, source_target_pairs={{0,20},{4,24},{8,28},{12,16},{16,36},{20,40},{24,44},{28,32},{32,5... | collective-permute-start | bytes 589832 | tf_op jit(solution)/shard_map/ppermute | solution.py:38
  148.5 3.6 %collective-permute-done.11.a3 = bf16[256,384]{1,0:T(8,128)(2,1)S(1)} collective-permute-done((bf16[256,384]{1,0:T(8,128)(2,1)S(1)}, bf16[256,384]{1,0:T(8,128)(2,1)S(1)}, u32[]{:S(2)}, u32[]{:S(2)}) %collective-permute-start.11) | collective-permute-done | bytes 196640 | tf_op jit(solution)/shard_map/ppermute | solution.py:38
  152.2 4.2 %collective-permute-done.8.a0 = bf16[256,384]{1,0:T(8,128)(2,1)S(1)} collective-permute-done((bf16[256,384]{1,0:T(8,128)(2,1)S(1)}, bf16[256,384]{1,0:T(8,128)(2,1)S(1)}, u32[]{:S(2)}, u32[]{:S(2)}) %collective-permute-start.8) | collective-permute-done | bytes 196640 | tf_op jit(solution)/shard_map/ppermute | solution.py:38
  156.3 4.7 %collective-permute-done.9.a1 = bf16[256,384]{1,0:T(8,128)(2,1)S(1)} collective-permute-done((bf16[256,384]{1,0:T(8,128)(2,1)S(1)}, bf16[256,384]{1,0:T(8,128)(2,1)S(1)}, u32[]{:S(2)}, u32[]{:S(2)}) %collective-permute-start.9) | collective-permute-done | bytes 196640 | tf_op jit(solution)/shard_map/ppermute | solution.py:38
  161.0 2.7 %out_cols.1.y0 = bf16[256,768]{1,0:T(8,128)(2,1)} custom-call(s32[3]{0:T(128)S(1)} %pad_add_fusion.sc, bf16[256,384]{1,0:T(8,128)(2,1)S(1)} %collective-permute-done.8.a0, bf16[256,384]{1,0:T(8,128)(2,1)S(1)} %collective-permute-done.9.a1, bf16[256,384]{1,0:T(8,128)(2,1)S(1)} %collective-permute-done.10.a2, bf16[256,384]{1,0:T(8,128)(2,1)S(1)} %collective-permute-done.11.a3, ...), custom_call_target="tpu_custom_call" | custom-call | tf_op jit(solution)/shard_map/out_cols/pallas_call | solution.py:284
  167.4 15.9 %collective-permute-done.20.y1 = bf16[256,768]{1,0:T(8,128)(2,1)} collective-permute-done((bf16[256,768]{1,0:T(8,128)(2,1)}, bf16[256,768]{1,0:T(8,128)(2,1)}, u32[]{:S(2)}, u32[]{:S(2)}) %collective-permute-start.20) | collective-permute-done | bytes 393248 | tf_op jit(solution)/shard_map/ppermute | solution.py:38
  186.1 8.0 %qkv_next.1 = (bf16[256,384]{1,0:T(8,128)(2,1)S(1)}, bf16[256,384]{1,0:T(8,128)(2,1)S(1)}, bf16[256,384]{1,0:T(8,128)(2,1)S(1)}, bf16[64,3072]{1,0:T(8,128)(2,1)}, bf16[64,3072]{1,0:T(8,128)(2,1)S(1)}) custom-call(s32[3]{0:T(128)S(1)} %pad_add_fusion.sc, bf16[256,768]{1,0:T(8,128)(2,1)} %out_cols.1.y0, bf16[256,768]{1,0:T(8,128)(2,1)} %collective-permute-done.20.y1, ...), custom_call_target="tpu_custom_call" | custom-call | tf_op jit(solution)/shard_map/qkv_next/pallas_call | solution.py:150
  196.6 7.1 %collective-permute-done.25.q_ref = bf16[256,384]{1,0:T(8,128)(2,1)S(1)} collective-permute-done((bf16[256,384]{1,0:T(8,128)(2,1)S(1)}, bf16[256,384]{1,0:T(8,128)(2,1)S(1)}, u32[]{:S(2)}, u32[]{:S(2)}) %collective-permute-start.25) | collective-permute-done | bytes 196640 | tf_op jit(solution)/shard_map/ppermute | solution.py:38
  203.7 6.6 %attend_other.3 = bf16[256,512]{1,0:T(8,128)(2,1)} custom-call(s32[3]{0:T(128)S(1)} %pad_add_fusion.sc, s32[1]{0:T(128)} %get-tuple-element.50.patch, bf16[256,384]{1,0:T(8,128)(2,1)S(1)} %collective-permute-done.25.q_ref, bf16[256,384]{1,0:T(8,128)(2,1)S(1)} %get-tuple-element.25.ko, bf16[256,384]{1,0:T(8,128)(2,1)S(1)} %get-tuple-element.26.vo, ...), custom_call_target="tpu_custom_call" | custom-call | tf_op jit(solution)/shard_map/attend_other/pallas_call | solution.py:215
  216.0 5.8 %attend_own.3 = (f32[256,384]{1,0:T(8,128)S(1)}, f32[256,128]{1,0:T(8,128)S(1)}) custom-call(s32[3]{0:T(128)S(1)} %pad_add_fusion.sc, s32[1]{0:T(128)} %get-tuple-element.50.patch, bf16[256,384]{1,0:T(8,128)(2,1)S(1)} %copy-done.17, bf16[256,384]{1,0:T(8,128)(2,1)S(1)} %copy-done.6, bf16[256,384]{1,0:T(8,128)(2,1)S(1)} %copy-done.8, ...), custom_call_target="tpu_custom_call" | custom-call | tf_op jit(solution)/shard_map/attend_own/pallas_call | solution.py:215
  229.2 3.3 %collective-permute-done.28.a2 = bf16[64,384]{1,0:T(8,128)(2,1)S(1)} collective-permute-done((bf16[64,384]{1,0:T(8,128)(2,1)S(1)}, bf16[64,384]{1,0:T(8,128)(2,1)S(1)}, u32[]{:S(2)}, u32[]{:S(2)}) %collective-permute-start.28) | collective-permute-done | bytes 49184 | tf_op jit(solution)/shard_map/ppermute | solution.py:38
  238.8 6.1 %out_last.1 = bf16[1,2,64,3072]{3,2,1,0:T(8,128)(2,1)} custom-call(s32[3]{0:T(128)S(1)} %pad_add_fusion.sc, bf16[64,384]{1,0:T(8,128)(2,1)S(1)} %copy-done.15, bf16[64,384]{1,0:T(8,128)(2,1)S(1)} %copy-done.19, bf16[64,384]{1,0:T(8,128)(2,1)S(1)} %copy-done.21, bf16[64,384]{1,0:T(8,128)(2,1)S(1)} %copy-done.23, bf16[1536,3072]{1,0:T(8,128)(2,1)} %bitcast.55, ...), custom_call_target="tpu_custom_call" | custom-call | tf_op jit(solution)/shard_map/out_last/pallas_call | solution.py:309
  (127 shorter events, 66.5 us)
Async XLA Ops:
  6.5 160.9 %all-gather.5.cloned.1.call-start = ((), (), s32[]{:S(2)}) async-start(), calls=%async_computation.1 | async-start | bytes 1966080 | tf_op jit(solution)/shard_map/all_gather | solution.py:376
  7.3 226.5 %all-gather.7.cloned.1.call-start = ((), (), s32[]{:S(2)}) async-start(), calls=%async_computation.2 | async-start | bytes 10027008 | tf_op jit(solution)/shard_map/all_gather | solution.py:377
  9.2 13.1 %collective-permute-start.12 = (bf16[96,768]{1,0:T(8,128)(2,1)S(1)}, bf16[96,768]{1,0:T(8,128)(2,1)S(1)}, u32[]{:S(2)}, u32[]{:S(2)}) collective-permute-start(bf16[96,768]{1,0:T(8,128)(2,1)S(1)} %get-tuple-element.36), channel_id=1, source_target_pairs={{0,16},{16,32},{32,48},{48,64},{64,80},{80,96},{96,112},{112,0},{1... | collective-permute-start | bytes 442376 | tf_op jit(solution)/shard_map/ppermute | solution.py:38
  10.9 12.9 %collective-permute-start.13 = (bf16[96,768]{1,0:T(8,128)(2,1)S(1)}, bf16[96,768]{1,0:T(8,128)(2,1)S(1)}, u32[]{:S(2)}, u32[]{:S(2)}) collective-permute-start(bf16[96,768]{1,0:T(8,128)(2,1)S(1)} %get-tuple-element.35), channel_id=1, source_target_pairs={{0,20},{4,24},{8,28},{12,16},{16,36},{20,40},{24,44},{28,32},{32,5... | collective-permute-start | bytes 442376 | tf_op jit(solution)/shard_map/ppermute | solution.py:38
  13.4 14.9 %collective-permute-start.14 = (bf16[96,768]{1,0:T(8,128)(2,1)S(1)}, bf16[96,768]{1,0:T(8,128)(2,1)S(1)}, u32[]{:S(2)}, u32[]{:S(2)}) collective-permute-start(bf16[96,768]{1,0:T(8,128)(2,1)S(1)} %get-tuple-element.34), channel_id=1, source_target_pairs={{0,24},{4,28},{8,16},{12,20},{16,40},{20,44},{24,32},{28,36},{32,5... | collective-permute-start | bytes 442376 | tf_op jit(solution)/shard_map/ppermute | solution.py:38
  22.4 85.9 %collective-permute-start.5 = (bf16[2,1024,384]{2,1,0:T(8,128)(2,1)}, bf16[2,1024,384]{2,1,0:T(8,128)(2,1)}, u32[]{:S(2)}, u32[]{:S(2)}) collective-permute-start(bf16[2,1024,384]{2,1,0:T(8,128)(2,1)} %bitcast.47.so), channel_id=1, source_target_pairs={{0,1},{1,0},{2,3},{3,2},{4,5},{5,4},{6,7},{7,6},{8,9},{9,8},{10,11... | collective-permute-start | bytes 4718600 | tf_op jit(solution)/shard_map/ppermute | solution.py:38
  29.5 16.0 %collective-permute-start.16 = (bf16[4,96,768]{2,1,0:T(8,128)(2,1)S(1)}, bf16[4,96,768]{2,1,0:T(8,128)(2,1)S(1)}, u32[]{:S(2)}, u32[]{:S(2)}) collective-permute-start(bf16[4,96,768]{2,1,0:T(8,128)(2,1)S(1)} %pad_maximum_fusion), channel_id=1, source_target_pairs={{0,2},{1,3},{2,0},{3,1},{4,6},{5,7},{6,4},{7,5},{8,10},{9,11},{10,... | collective-permute-start | bytes 1769480 | tf_op jit(solution)/shard_map/ppermute | solution.py:38
  46.6 89.1 %collective-permute-start.17 = (bf16[8,96,768]{2,1,0:T(8,128)(2,1)}, bf16[8,96,768]{2,1,0:T(8,128)(2,1)}, u32[]{:S(2)}, u32[]{:S(2)}) collective-permute-start(bf16[8,96,768]{2,1,0:T(8,128)(2,1)} %get-tuple-element.31), channel_id=1, source_target_pairs={{0,1},{1,0},{2,3},{3,2},{4,5},{5,4},{6,7},{7,6},{8,9},{9,8},{10,11... | collective-permute-start | bytes 3538952 | tf_op jit(solution)/shard_map/ppermute | solution.py:38
  46.6 37.7 %collective-permute-start = (bf16[64,3072]{1,0:T(8,128)(2,1)}, bf16[64,3072]{1,0:T(8,128)(2,1)}, u32[]{:S(2)}, u32[]{:S(2)}) collective-permute-start(bf16[64,3072]{1,0:T(8,128)(2,1)} %bitcast.3.x0), channel_id=1, source_target_pairs={{0,4},{4,8},{8,12},{12,0},{1,5},{5,9},{9,13},{13,1},{2,6},{6,10},{... | collective-permute-start | bytes 1179656 | tf_op jit(solution)/shard_map/ppermute | solution.py:38
  47.3 37.0 %collective-permute-start.1 = (bf16[64,3072]{1,0:T(8,128)(2,1)}, bf16[64,3072]{1,0:T(8,128)(2,1)}, u32[]{:S(2)}, u32[]{:S(2)}) collective-permute-start(bf16[64,3072]{1,0:T(8,128)(2,1)} %bitcast.3.x0), channel_id=1, source_target_pairs={{0,8},{4,12},{8,0},{12,4},{1,9},{5,13},{9,1},{13,5},{2,10},{6,14},... | collective-permute-start | bytes 1179656 | tf_op jit(solution)/shard_map/ppermute | solution.py:38
  49.0 35.3 %collective-permute-start.2 = (bf16[64,3072]{1,0:T(8,128)(2,1)}, bf16[64,3072]{1,0:T(8,128)(2,1)}, u32[]{:S(2)}, u32[]{:S(2)}) collective-permute-start(bf16[64,3072]{1,0:T(8,128)(2,1)} %bitcast.3.x0), channel_id=1, source_target_pairs={{0,12},{4,0},{8,4},{12,8},{1,13},{5,1},{9,5},{13,9},{2,14},{6,2},{... | collective-permute-start | bytes 1179656 | tf_op jit(solution)/shard_map/ppermute | solution.py:38
  53.9 27.4 %all-to-all-start = ((f32[16,3,192]{2,1,0:T(4,128)}), f32[16,3,192]{2,1,0:T(4,128)}, u32[]{:S(2)}, u32[]{:S(2)}) async-start(f32[16,3,192]{2,1,0:T(4,128)} %broadcast_in_dim.2), calls=%async_computation | async-start | bytes 131072 | tf_op jit(solution)/shard_map/all_to_all | solution.py:354
  94.8 13.5 %collective-permute-start.6 = (bf16[256,384]{1,0:T(8,128)(2,1)}, bf16[256,384]{1,0:T(8,128)(2,1)}, u32[]{:S(2)}, u32[]{:S(2)}) collective-permute-start(bf16[256,384]{1,0:T(8,128)(2,1)} %get-tuple-element.18.q_ref), channel_id=1, source_target_pairs={{0,2},{1,3},{2,0},{3,1},{4,6},{5,7},{6,4},{7,5},{8,10},{9,11},{10,... | collective-permute-start | bytes 589832 | tf_op jit(solution)/shard_map/ppermute | solution.py:38
  115.3 18.2 %collective-permute-start.7 = (bf16[256,512]{1,0:T(8,128)(2,1)}, bf16[256,512]{1,0:T(8,128)(2,1)}, u32[]{:S(2)}, u32[]{:S(2)}) collective-permute-start(bf16[256,512]{1,0:T(8,128)(2,1)} %attend_other.2), channel_id=1, source_target_pairs={{0,2},{1,3},{2,0},{3,1},{4,6},{5,7},{6,4},{7,5},{8,10},{9,11},{10,... | collective-permute-start | bytes 786440 | tf_op jit(solution)/shard_map/ppermute | solution.py:38
  115.4 33.2 %collective-permute-start.18 = (bf16[256,768]{1,0:T(8,128)(2,1)}, bf16[256,768]{1,0:T(8,128)(2,1)}, u32[]{:S(2)}, u32[]{:S(2)}) collective-permute-start(bf16[256,768]{1,0:T(8,128)(2,1)} %get-tuple-element.23), channel_id=1, source_target_pairs={{0,16},{16,32},{32,48},{48,64},{64,80},{80,96},{96,112},{112,0},{1... | collective-permute-start | bytes 1179656 | tf_op jit(solution)/shard_map/ppermute | solution.py:38
  117.6 18.0 %collective-permute-start.19 = (f32[1,3072]{1,0:T(1,128)S(1)}, f32[1,3072]{1,0:T(1,128)}, u32[]{:S(2)}, u32[]{:S(2)}) collective-permute-start(f32[1,3072]{1,0:T(1,128)S(1)} %slice.7), channel_id=1, source_target_pairs={{0,16},{16,32},{32,48},{48,64},{64,80},{80,96},{96,112},{112,0},{1... | collective-permute-start | bytes 36872 | tf_op jit(solution)/shard_map/ppermute | solution.py:38
  135.5 13.1 %collective-permute-start.10 = (bf16[256,384]{1,0:T(8,128)(2,1)S(1)}, bf16[256,384]{1,0:T(8,128)(2,1)S(1)}, u32[]{:S(2)}, u32[]{:S(2)}) collective-permute-start(bf16[256,384]{1,0:T(8,128)(2,1)S(1)} %merge.2), channel_id=1, source_target_pairs={{0,24},{4,28},{8,16},{12,20},{16,40},{20,44},{24,32},{28,36},{32,5... | collective-permute-start | bytes 589832 | tf_op jit(solution)/shard_map/ppermute | solution.py:38
  135.5 16.6 %collective-permute-start.11 = (bf16[256,384]{1,0:T(8,128)(2,1)S(1)}, bf16[256,384]{1,0:T(8,128)(2,1)S(1)}, u32[]{:S(2)}, u32[]{:S(2)}) collective-permute-start(bf16[256,384]{1,0:T(8,128)(2,1)S(1)} %merge.2), channel_id=1, source_target_pairs={{0,28},{4,16},{8,20},{12,24},{16,44},{20,32},{24,36},{28,40},{32,6... | collective-permute-start | bytes 589832 | tf_op jit(solution)/shard_map/ppermute | solution.py:38
  135.6 20.7 %collective-permute-start.8 = (bf16[256,384]{1,0:T(8,128)(2,1)S(1)}, bf16[256,384]{1,0:T(8,128)(2,1)S(1)}, u32[]{:S(2)}, u32[]{:S(2)}) collective-permute-start(bf16[256,384]{1,0:T(8,128)(2,1)S(1)} %merge.2), channel_id=1, source_target_pairs={{0,16},{16,32},{32,48},{48,64},{64,80},{80,96},{96,112},{112,0},{1... | collective-permute-start | bytes 589832 | tf_op jit(solution)/shard_map/ppermute | solution.py:38
  135.7 25.3 %collective-permute-start.9 = (bf16[256,384]{1,0:T(8,128)(2,1)S(1)}, bf16[256,384]{1,0:T(8,128)(2,1)S(1)}, u32[]{:S(2)}, u32[]{:S(2)}) collective-permute-start(bf16[256,384]{1,0:T(8,128)(2,1)S(1)} %merge.2), channel_id=1, source_target_pairs={{0,20},{4,24},{8,28},{12,16},{16,36},{20,40},{24,44},{28,32},{32,5... | collective-permute-start | bytes 589832 | tf_op jit(solution)/shard_map/ppermute | solution.py:38
  163.7 19.6 %collective-permute-start.20 = (bf16[256,768]{1,0:T(8,128)(2,1)}, bf16[256,768]{1,0:T(8,128)(2,1)}, u32[]{:S(2)}, u32[]{:S(2)}) collective-permute-start(bf16[256,768]{1,0:T(8,128)(2,1)} %out_cols.1.y0), channel_id=1, source_target_pairs={{0,4},{4,8},{8,12},{12,0},{1,5},{5,9},{9,13},{13,1},{2,6},{6,10},{... | collective-permute-start | bytes 1179656 | tf_op jit(solution)/shard_map/ppermute | solution.py:38
  163.7 19.6 %collective-permute-start.21 = (bf16[256,768]{1,0:T(8,128)(2,1)}, bf16[256,768]{1,0:T(8,128)(2,1)}, u32[]{:S(2)}, u32[]{:S(2)}) collective-permute-start(bf16[256,768]{1,0:T(8,128)(2,1)} %out_cols.1.y0), channel_id=1, source_target_pairs={{0,8},{4,12},{8,0},{12,4},{1,9},{5,13},{9,1},{13,5},{2,10},{6,14},... | collective-permute-start | bytes 1179656 | tf_op jit(solution)/shard_map/ppermute | solution.py:38
  166.0 18.0 %collective-permute-start.22 = (bf16[256,768]{1,0:T(8,128)(2,1)}, bf16[256,768]{1,0:T(8,128)(2,1)}, u32[]{:S(2)}, u32[]{:S(2)}) collective-permute-start(bf16[256,768]{1,0:T(8,128)(2,1)} %out_cols.1.y0), channel_id=1, source_target_pairs={{0,12},{4,0},{8,4},{12,8},{1,13},{5,1},{9,5},{13,9},{2,14},{6,2},{... | collective-permute-start | bytes 1179656 | tf_op jit(solution)/shard_map/ppermute | solution.py:38
  211.3 16.4 %collective-permute-start.30 = (bf16[64,3072]{1,0:T(8,128)(2,1)}, bf16[64,3072]{1,0:T(8,128)(2,1)}, u32[]{:S(2)}, u32[]{:S(2)}) collective-permute-start(bf16[64,3072]{1,0:T(8,128)(2,1)} %get-tuple-element.30), channel_id=1, source_target_pairs={{0,112},{16,0},{32,16},{48,32},{64,48},{80,64},{96,80},{112,96},{1... | collective-permute-start | bytes 1179656 | tf_op jit(solution)/shard_map/ppermute | solution.py:38
  (35 other events, 170.7 us)
Sparse Core Ops, SparseCore 0:
  9.0 32.4 all-gather.4
  43.9 97.3 all-gather.6
